TPU v7x, 32 devices: a whole 2x2x4 slice. The times are simulated.
32 devices in a mesh: row: 4 (over x, core), col: 8 (over z, y).
Axes of the slice: x: 2, y: 2, z: 4, core: 2. Of those that a mesh axis runs over, the one named last changes fastest.
Arguments:
- kernel: float32 [8192, 8192], P('row', 'col'), as said below
Outputs:
- schur: float32 [8192, 8192], P('row', 'col')
- panels: float32 [8192, 768], P('row')
Inputs may be any that keep to these rules, and one draw needn't show every extreme that they name: kernel is symmetric and positive definite with smallest eigenvalue of order one.
All inputs are finite; a program needn't handle non-finite values.
Results may differ from a plain program's by a relative error of at most 0.00027.
Values sent between devices are 32-bit elements; how exact they have to be, the bound alone decides.
A program may use at most 128 MiB of HBM per device.

v0:
```python
import jax
import jax.numpy as jnp
from jax import lax
from jax.sharding import PartitionSpec as P

BLOCK = 256
STEPS = 3


def spread(array, axis, root):
    mine = lax.axis_index(axis) == root
    return lax.psum(jnp.where(mine, array, jnp.zeros_like(array)), axis)


def place(factor, column, block_ids, step):
    solved = jax.scipy.linalg.solve_triangular(factor, column.T, lower=True).T
    tiled = jnp.tile(factor, (column.shape[0] // factor.shape[0], 1))
    inner = jnp.where((block_ids == step)[:, None], tiled, jnp.float32(0.0))
    return jnp.where((block_ids > step)[:, None], solved, inner)


def pick(panel, col_index, row_count, col_blocks):
    width = panel.shape[1]
    groups = panel.shape[0] // width // col_blocks
    grouped = panel.reshape(col_blocks, groups, width, width)
    chosen = lax.dynamic_index_in_dim(grouped, col_index // row_count, 1, keepdims=False)
    return chosen.reshape(col_blocks * width, width)


def shards(kernel):
    row_count = lax.axis_size("row")
    col_count = lax.axis_size("col")
    row_index = lax.axis_index("row")
    col_index = lax.axis_index("col")
    rows_local, cols_local = kernel.shape
    col_blocks = cols_local // BLOCK
    row_ids = jnp.arange(rows_local) // BLOCK * row_count + row_index
    col_ids = jnp.arange(cols_local) // BLOCK * col_count + col_index
    matrix = kernel
    collected = []
    for step in range(STEPS):
        row_root = step % row_count
        row_slot = step // row_count
        col_root = step % col_count
        col_slot = step // col_count
        corner = matrix[
            row_slot * BLOCK : (row_slot + 1) * BLOCK, col_slot * BLOCK : (col_slot + 1) * BLOCK
        ]
        factor = jnp.linalg.cholesky(corner)
        column = matrix[:, col_slot * BLOCK : (col_slot + 1) * BLOCK]
        factor = spread(factor, "row", row_root)
        panel = spread(place(factor, column, row_ids, step), "col", col_root)
        across = spread(pick(panel, col_index, row_count, col_blocks), "row", col_index % row_count)
        collected.append(panel)
        update = lax.dot_general(
            panel,
            across,
            (((1,), (1,)), ((), ())),
            precision=lax.Precision.HIGHEST,
            preferred_element_type=jnp.float32,
        )
        matrix = matrix - update
    keep = (row_ids >= STEPS)[:, None] & (col_ids >= STEPS)[None, :]
    schur = jnp.where(keep, matrix, jnp.float32(0.0))
    return (schur, jnp.concatenate(collected, axis=1))


def solution(mesh):
    return jax.shard_map(
        shards,
        mesh=mesh,
        in_specs=(P("row", "col"),),
        out_specs=(P("row", "col"), P("row", None)),
        check_vma=False,
    )
```

profile of v0, /device:TPU:24, one launch (start us, length us, event | category | flops | bytes accessed | tf_op | source)
XLA Modules:
  0.0 829.7 jit_solution(14348636954789965284)
XLA Ops:
  7.2 9.1 %copy.6 = f32[2048,1024]{0,1:T(8,128)} copy(f32[2048,1024]{1,0:T(8,128)} %param.4) | data formatting | bytes 16777216 | tf_op args[0]
  18.5 11.7 %cholesky.172 = f32[128,128]{1,0:T(8,128)S(1)} custom-call(f32[128,128]{1,0:T(8,128)S(1)} %cholesky.270), custom_call_target="Cholesky" | custom-call | tf_op jit(solution)/shard_map/jit(cholesky)/cholesky | solution.py:49
  30.2 9.8 %custom-call.15 = f32[1,128,128]{1,2,0:T(8,128)S(1)} custom-call(f32[1,128,128]{2,1,0:T(8,128)S(1)} %get-tuple-element.70), custom_call_target="InvertDiagBlocksLowerTriangular" | custom-call | tf_op jit(solution)/shard_map/jit(cholesky)/cholesky | solution.py:49
  40.5 11.7 %cholesky.189 = f32[128,128]{1,0:T(8,128)S(1)} custom-call(f32[128,128]{1,0:T(8,128)S(1)} %convolution_subtract_fusion.7), custom_call_target="Cholesky" | custom-call | tf_op jit(solution)/shard_map/jit(cholesky)/cholesky | solution.py:49
  57.1 31.1 %all-reduce.11.cloned.1.call-done = f32[256,256]{1,0:T(8,128)} async-done(((f32[256,256]{1,0:T(8,128)}), f32[256,256]{1,0:T(8,128)}) %all-reduce.11.cloned.1.call-update) | async-done | bytes 262160 | tf_op jit(solution)/shard_map/psum | solution.py:12
  89.3 4.0 while.6
  93.3 19.7 %custom-call.16 = f32[2,128,128]{1,2,0:T(8,128)S(1)} custom-call(f32[2,128,128]{2,1,0:T(8,128)S(1)} %get-tuple-element.24), custom_call_target="InvertDiagBlocksLowerTriangular" | custom-call | tf_op jit(solution)/shard_map/jit(_solve_triangular)/triangular_solve | solution.py:16
  114.0 1.8 convolution_subtract_fusion.4
  120.3 100.2 %all-reduce.13.cloned.1.call-done = f32[2048,256]{0,1:T(8,128)} async-done(((f32[2048,256]{0,1:T(8,128)}), f32[2048,256]{0,1:T(8,128)}) %all-reduce.13.cloned.1.call-update) | async-done | bytes 2097168 | tf_op jit(solution)/shard_map/psum | solution.py:12
  220.5 3.0 reshape.105
  223.6 3.3 fusion.6
  228.2 37.2 %all-reduce.15.cloned.1.call-done = f32[1024,256]{0,1:T(8,128)} async-done(((f32[1024,256]{0,1:T(8,128)}), f32[1024,256]{0,1:T(8,128)}) %all-reduce.15.cloned.1.call-update) | async-done | bytes 1048592 | tf_op jit(solution)/shard_map/psum | solution.py:12
  265.4 10.6 %convolution_subtract_fusion.1 = f32[2048,1024]{0,1:T(8,128)S(1)} fusion(f32[2048,1024]{0,1:T(8,128)} %copy.6, f32[2048,256]{0,1:T(8,128)S(1)} %copy-done.2, f32[1024,256]{0,1:T(8,128)} %all-reduce.15.cloned.1.call-done), kind=kOutput, calls=%fused_computation.9 | convolution fusion | flops 6444548096 | bytes 19922944 | tf_op jit(solution)/shard_map/dot_general | solution.py:55
  276.0 3.4 copy-done
  280.5 11.7 %cholesky.206 = f32[128,128]{1,0:T(8,128)S(1)} custom-call(f32[128,128]{1,0:T(8,128)S(1)} %cholesky.273), custom_call_target="Cholesky" | custom-call | tf_op jit(solution)/shard_map/jit(cholesky)/cholesky | solution.py:49
  292.3 9.8 %custom-call.17 = f32[1,128,128]{1,2,0:T(8,128)S(1)} custom-call(f32[1,128,128]{2,1,0:T(8,128)S(1)} %get-tuple-element.66), custom_call_target="InvertDiagBlocksLowerTriangular" | custom-call | tf_op jit(solution)/shard_map/jit(cholesky)/cholesky | solution.py:49
  302.6 11.7 %cholesky.223 = f32[128,128]{1,0:T(8,128)S(1)} custom-call(f32[128,128]{1,0:T(8,128)S(1)} %convolution_subtract_fusion.6), custom_call_target="Cholesky" | custom-call | tf_op jit(solution)/shard_map/jit(cholesky)/cholesky | solution.py:49
  317.9 3.1 slice_bitcast_fusion.1
  321.0 29.3 %all-reduce.17.cloned.1.call-done = f32[256,256]{1,0:T(8,128)} async-done(((f32[256,256]{1,0:T(8,128)}), f32[256,256]{1,0:T(8,128)}) %all-reduce.17.cloned.1.call-update) | async-done | bytes 262160 | tf_op jit(solution)/shard_map/psum | solution.py:12
  351.3 4.5 while.7
  355.7 19.7 %custom-call.18 = f32[2,128,128]{1,2,0:T(8,128)S(1)} custom-call(f32[2,128,128]{2,1,0:T(8,128)S(1)} %get-tuple-element.25), custom_call_target="InvertDiagBlocksLowerTriangular" | custom-call | tf_op jit(solution)/shard_map/jit(_solve_triangular)/triangular_solve | solution.py:16
  375.4 2.4 fusion.11
  378.9 2.0 fusion.28
  383.4 1.8 fusion.3
  385.2 100.7 %all-reduce.19.cloned.1.call-done = f32[2048,256]{0,1:T(8,128)} async-done(((f32[2048,256]{0,1:T(8,128)}), f32[2048,256]{0,1:T(8,128)}) %all-reduce.19.cloned.1.call-update) | async-done | bytes 2097168 | tf_op jit(solution)/shard_map/psum | solution.py:12
  485.9 4.0 reshape.106
  489.9 5.0 fusion.7
  496.1 37.2 %all-reduce.21.cloned.1.call-done = f32[1024,256]{0,1:T(8,128)} async-done(((f32[1024,256]{0,1:T(8,128)}), f32[1024,256]{0,1:T(8,128)}) %all-reduce.21.cloned.1.call-update) | async-done | bytes 1048592 | tf_op jit(solution)/shard_map/psum | solution.py:12
  533.3 10.7 %convolution_subtract_fusion = f32[2048,1024]{0,1:T(8,128)S(1)} fusion(f32[2048,1024]{0,1:T(8,128)} %copy-done, f32[2048,256]{0,1:T(8,128)} %all-reduce.19.cloned.1.call-done, f32[1024,256]{0,1:T(8,128)} %all-reduce.21.cloned.1.call-done), kind=kOutput, calls=%fused_computation.8 | convolution fusion | flops 6444548096 | bytes 19922944 | tf_op jit(solution)/shard_map/dot_general | solution.py:55
  544.0 3.4 copy-done.1
  548.6 11.7 %cholesky.240 = f32[128,128]{1,0:T(8,128)S(1)} custom-call(f32[128,128]{1,0:T(8,128)S(1)} %cholesky.276), custom_call_target="Cholesky" | custom-call | tf_op jit(solution)/shard_map/jit(cholesky)/cholesky | solution.py:49
  560.3 9.8 %custom-call.19 = f32[1,128,128]{1,2,0:T(8,128)S(1)} custom-call(f32[1,128,128]{2,1,0:T(8,128)S(1)} %get-tuple-element.62), custom_call_target="InvertDiagBlocksLowerTriangular" | custom-call | tf_op jit(solution)/shard_map/jit(cholesky)/cholesky | solution.py:49
  570.6 11.7 %cholesky.257 = f32[128,128]{1,0:T(8,128)S(1)} custom-call(f32[128,128]{1,0:T(8,128)S(1)} %convolution_subtract_fusion.5), custom_call_target="Cholesky" | custom-call | tf_op jit(solution)/shard_map/jit(cholesky)/cholesky | solution.py:49
  585.7 3.1 slice_bitcast_fusion
  588.9 29.3 %all-reduce.23.cloned.1.call-done = f32[256,256]{1,0:T(8,128)} async-done(((f32[256,256]{1,0:T(8,128)}), f32[256,256]{1,0:T(8,128)}) %all-reduce.23.cloned.1.call-update) | async-done | bytes 262160 | tf_op jit(solution)/shard_map/psum | solution.py:12
  619.2 4.3 while.8
  623.4 19.7 %custom-call.20 = f32[2,128,128]{1,2,0:T(8,128)S(1)} custom-call(f32[2,128,128]{2,1,0:T(8,128)S(1)} %get-tuple-element.26), custom_call_target="InvertDiagBlocksLowerTriangular" | custom-call | tf_op jit(solution)/shard_map/jit(_solve_triangular)/triangular_solve | solution.py:16
  643.1 2.4 fusion.9
  646.6 2.0 fusion.24
  651.1 1.8 fusion.5
  652.9 100.6 %all-reduce.25.cloned.1.call-done = f32[2048,256]{0,1:T(8,128)} async-done(((f32[2048,256]{0,1:T(8,128)}), f32[2048,256]{0,1:T(8,128)}) %all-reduce.25.cloned.1.call-update) | async-done | bytes 2097168 | tf_op jit(solution)/shard_map/psum | solution.py:12
  753.5 4.2 reshape.107
  757.7 5.0 fusion.8
  763.9 5.7 pad_maximum_fusion
  769.5 6.9 copy.15
  776.4 24.7 %all-reduce.27.cloned.1.call-done = f32[1024,256]{0,1:T(8,128)} async-done(((f32[1024,256]{0,1:T(8,128)}), f32[1024,256]{0,1:T(8,128)}) %all-reduce.27.cloned.1.call-update) | async-done | bytes 1048592 | tf_op jit(solution)/shard_map/psum | solution.py:12
  801.1 12.4 %subtract_select_fusion = f32[2048,1024]{0,1:T(8,128)} fusion(f32[2048,1024]{0,1:T(8,128)} %copy-done.1, f32[2048,256]{0,1:T(8,128)S(1)} %copy-done.3, f32[1024,256]{0,1:T(8,128)} %all-reduce.27.cloned.1.call-done, pred[2048]{0:T(1024)(128)(4,1)S(1)} %fusion.48, pred[1024]{0:T(1024)(128)(4,1)S(1)} %fusion.52), kind=kOutput, calls=%fused_computation.6 | convolution fusion | flops 6448742400 | bytes 19926016 | tf_op jit(solution)/shard_map/dot_general | solution.py:55
  813.4 9.2 %copy.14 = f32[2048,1024]{1,0:T(8,128)} copy(f32[2048,1024]{0,1:T(8,128)} %subtract_select_fusion) | data formatting | bytes 16777216
  (118 shorter events, 44.9 us)
Async XLA Ops:
  7.2 81.0 %all-reduce.11.cloned.1.call-start = ((), (), s32[]{:S(2)}) async-start(), calls=%async_computation | async-start | bytes 524288 | tf_op jit(solution)/shard_map/psum | solution.py:12
  55.1 165.4 %all-reduce.13.cloned.1.call-start = ((), (), s32[]{:S(2)}) async-start(), calls=%async_computation.1 | async-start | bytes 4194304 | tf_op jit(solution)/shard_map/psum | solution.py:12
  115.8 1.1 copy-start.8
  119.8 145.5 %all-reduce.15.cloned.1.call-start = ((), (), s32[]{:S(2)}) async-start(), calls=%async_computation.2 | async-start | bytes 2097152 | tf_op jit(solution)/shard_map/psum | solution.py:12
  226.9 38.5 %copy-start.2 = (f32[2048,256]{0,1:T(8,128)S(1)}, f32[2048,256]{0,1:T(8,128)}, u32[]{:S(2)}) copy-start(f32[2048,256]{0,1:T(8,128)} %all-reduce.13.cloned.1.call-done) | copy-start | bytes 6291460
  228.1 122.2 %all-reduce.17.cloned.1.call-start = ((), (), s32[]{:S(2)}) async-start(), calls=%async_computation.3 | async-start | bytes 524288 | tf_op jit(solution)/shard_map/psum | solution.py:12
  276.0 3.4 copy-start
  317.8 168.1 %all-reduce.19.cloned.1.call-start = ((), (), s32[]{:S(2)}) async-start(), calls=%async_computation.4 | async-start | bytes 4194304 | tf_op jit(solution)/shard_map/psum | solution.py:12
  375.4 2.4 copy-start.5
  382.1 1.2 copy-start.6
  385.2 148.1 %all-reduce.21.cloned.1.call-start = ((), (), s32[]{:S(2)}) async-start(), calls=%async_computation.5 | async-start | bytes 2097152 | tf_op jit(solution)/shard_map/psum | solution.py:12
  496.0 122.2 %all-reduce.23.cloned.1.call-start = ((), (), s32[]{:S(2)}) async-start(), calls=%async_computation.6 | async-start | bytes 524288 | tf_op jit(solution)/shard_map/psum | solution.py:12
  544.0 3.4 copy-start.1
  585.7 167.8 %all-reduce.25.cloned.1.call-start = ((), (), s32[]{:S(2)}) async-start(), calls=%async_computation.7 | async-start | bytes 4194304 | tf_op jit(solution)/shard_map/psum | solution.py:12
  643.1 2.4 copy-start.4
  649.8 1.2 copy-start.7
  652.9 148.2 %all-reduce.27.cloned.1.call-start = ((), (), s32[]{:S(2)}) async-start(), calls=%async_computation.8 | async-start | bytes 2097152 | tf_op jit(solution)/shard_map/psum | solution.py:12
  769.5 31.6 %copy-start.3 = (f32[2048,256]{0,1:T(8,128)S(1)}, f32[2048,256]{0,1:T(8,128)}, u32[]{:S(2)}) copy-start(f32[2048,256]{0,1:T(8,128)} %all-reduce.25.cloned.1.call-done) | copy-start | bytes 6291460
Sparse Core Ops, SparseCore 0:
  55.2 32.9 all-reduce.10
  120.0 100.5 all-reduce.12
  228.2 37.0 all-reduce.14
  317.9 32.3 all-reduce.16
  385.3 100.5 all-reduce.18
  496.1 37.0 all-reduce.20
  585.8 32.3 all-reduce.22
  653.0 100.4 all-reduce.24
  763.9 37.0 all-reduce.26
where the time goes:
time: 840 us; the launch traced here: 830 us
  waiting for transfers between devices  490 us (58%)
  other arithmetic  195 us (23%)
  local copies, waits for them, and re-layouts  74.3 us (9%)
  matrix products  49.9 us (6%)
  between operations  18.8 us (2%)
    psum x9, waiting for transfers between devices, spread(): return lax.psum(jnp.where(mine, array, jnp.zeros_like(array)), axis)  490 us
    another operation x20, other arithmetic, shards(): factor = jnp.linalg.cholesky(corner)  103 us
    another operation x7, other arithmetic, place(): solved = jax.scipy.linalg.solve_triangular(factor, column.T, lower=True).T  61.9 us
    unnamed x27, local copies, waits for them, and re-layouts  38.8 us
    dot_general x3, matrix products, shards(): lax.dot_general(panel, across, (((1,), (1,)), ((), ())), precision=lax.Pr...  33.7 us
    select_n x9, other arithmetic, spread(): return lax.psum(jnp.where(mine, array, jnp.zeros_like(array)), axis)  20.7 us
  transfers between devices with their start and end apart: 9, of which 9 were waited for; matrix products, arithmetic and copies ran while one was open for 2% of the time, Pallas kernels for 0%

commit v1 on v0

v1 whole, which is shorter than its diff:
```python
import functools

import jax
import jax.numpy as jnp
from jax import lax
from jax.experimental import pallas as pl
from jax.experimental.pallas import tpu as pltpu
from jax.sharding import PartitionSpec as P

BLOCK = 256
STEPS = 3
EDGE = STEPS * BLOCK
BASE = 128
CHUNK = 128
MESH = pl.DeviceIdType.MESH


def line_width(col_count):
    width = 1
    while 4 * width * width <= col_count:
        width *= 2
    return width


def gather_kernel(row_count, col_count, m_ref, a_ref, r_ref, c_ref, slab_send, slab_recv, edge_send, edge_recv,
                  corner_send, corner_recv, local_sem):
    width = line_width(col_count)
    depth = col_count // width
    rows = m_ref.shape[0]
    chunks = rows // CHUNK
    rounds = chunks // width
    lead = BLOCK // CHUNK
    p = lax.axis_index("row")
    q = lax.axis_index("col")
    a = q // width
    b = q % width

    barrier = pltpu.get_barrier_semaphore()
    for other in range(1, col_count):
        pl.semaphore_signal(barrier, inc=1, device_id=(p, lax.rem(q + other, col_count)), device_id_type=MESH)
    for other in range(1, row_count):
        pl.semaphore_signal(barrier, inc=1, device_id=(lax.rem(p + other, row_count), q), device_id_type=MESH)
    pl.semaphore_wait(barrier, col_count + row_count - 2)

    def slab_copy(k, chunk, way, own, device):
        start = pl.multiple_of(chunk * CHUNK, CHUNK)
        dst = a_ref.at[pl.ds(start, CHUNK), pl.ds(k * BLOCK, BLOCK)]
        src = m_ref.at[pl.ds(start, CHUNK), pl.ds(0, BLOCK)] if own else dst
        return pltpu.make_async_remote_copy(
            src_ref=src,
            dst_ref=dst,
            send_sem=slab_send.at[k, chunk, way],
            recv_sem=slab_recv.at[k, chunk],
            device_id=(p, device),
            device_id_type=MESH,
        )

    def forward(k, chunk, act):
        a0, b0 = k // width, k % width
        part = chunk % width
        mine = part == b

        @pl.when(q == k)
        def _():
            for other in range(width):
                if other != b0:
                    act(slab_copy(k, chunk, 2 + other, True, a0 * width + other))

            @pl.when(mine)
            def _():
                if a0 + 1 < depth:
                    act(slab_copy(k, chunk, 0, True, q + width))
                if a0 > 0:
                    act(slab_copy(k, chunk, 1, True, q - width))

        @pl.when(jnp.logical_and(q != k, mine))
        def _():
            @pl.when(jnp.logical_and(a >= a0, a + 1 < depth))
            def _():
                act(slab_copy(k, chunk, 0, False, q + width))

            @pl.when(jnp.logical_and(a <= a0, a > 0))
            def _():
                act(slab_copy(k, chunk, 1, False, q - width))

            @pl.when(a != a0)
            def _():
                for other in range(1, width):
                    to = lax.rem(b + other, width)
                    act(slab_copy(k, chunk, 2 + to, False, a * width + to))

    def arrive(k, chunk):
        slab_copy(k, chunk, 0, False, q).wait_recv()

    for k in range(STEPS):
        @pl.when(q == k)
        def _():
            pltpu.make_async_copy(
                m_ref.at[:, pl.ds(0, BLOCK)], a_ref.at[:, pl.ds(k * BLOCK, BLOCK)], local_sem.at[0]
            ).start()

            @pl.loop(0, chunks)
            def _(chunk):
                forward(k, chunk, lambda copy: copy.start())

    def relay(step):
        for k in range(STEPS):
            chunk = step * width + b

            @pl.when(q != k)
            def _():
                arrive(k, chunk)
                forward(k, chunk, lambda copy: copy.start())

    def rest(step):
        for k in range(STEPS):
            for other in range(1, width):
                chunk = step * width + lax.rem(b + other, width)

                @pl.when(q != k)
                def _():
                    arrive(k, chunk)

    lead_rounds = -(-lead // width)
    for step in range(lead_rounds):
        relay(jnp.int32(step))
        rest(jnp.int32(step))
    for k in range(STEPS):
        @pl.when(q == k)
        def _():
            pltpu.make_async_copy(
                m_ref.at[:, pl.ds(0, BLOCK)], a_ref.at[:, pl.ds(k * BLOCK, BLOCK)], local_sem.at[0]
            ).wait()

    def corner_copy(i, other):
        return pltpu.make_async_remote_copy(
            src_ref=a_ref.at[pl.ds(0, BLOCK), pl.ds(0, (i + 1) * BLOCK)],
            dst_ref=c_ref.at[pl.ds(i * BLOCK, BLOCK), pl.ds(0, (i + 1) * BLOCK)],
            send_sem=corner_send.at[other],
            recv_sem=corner_recv.at[i],
            device_id=(lax.rem(p + other, row_count), q),
            device_id_type=MESH,
        )

    def edge_copy(i, other):
        return pltpu.make_async_remote_copy(
            src_ref=m_ref.at[pl.ds(0, BLOCK), :],
            dst_ref=r_ref.at[pl.ds(i * BLOCK, BLOCK), :],
            send_sem=edge_send.at[other],
            recv_sem=edge_recv.at[i],
            device_id=(lax.rem(p + other, row_count), q),
            device_id_type=MESH,
        )

    def local_corner(i):
        return pltpu.make_async_copy(
            a_ref.at[pl.ds(0, BLOCK), pl.ds(0, (i + 1) * BLOCK)],
            c_ref.at[pl.ds(i * BLOCK, BLOCK), pl.ds(0, (i + 1) * BLOCK)],
            local_sem.at[1],
        )

    def local_edge(i):
        return pltpu.make_async_copy(
            m_ref.at[pl.ds(0, BLOCK), :], r_ref.at[pl.ds(i * BLOCK, BLOCK), :], local_sem.at[2]
        )

    for i in range(STEPS):
        @pl.when(p == i)
        def _():
            local_corner(i).start()
            local_edge(i).start()
            for other in range(1, row_count):
                corner_copy(i, other).start()
            for other in range(1, row_count):
                edge_copy(i, other).start()

    @pl.loop(lead_rounds, rounds)
    def _(step):
        relay(step)

    @pl.loop(lead_rounds, rounds)
    def _(step):
        rest(step)

    for i in range(STEPS):
        @pl.when(p == i)
        def _():
            local_corner(i).wait()
            local_edge(i).wait()
            for other in range(1, row_count):
                corner_copy(i, other).wait_send()
                edge_copy(i, other).wait_send()

        @pl.when(p != i)
        def _():
            corner_copy(i, 1).wait_recv()
            edge_copy(i, 1).wait_recv()

    for k in range(STEPS):
        @pl.loop(0, chunks)
        def _(chunk):
            forward(k, chunk, lambda copy: copy.wait_send())


def gather(kernel, row_count, col_count):
    rows, cols = kernel.shape
    width = line_width(col_count)
    chunks = rows // CHUNK
    return pl.pallas_call(
        functools.partial(gather_kernel, row_count, col_count),
        out_shape=(
            jax.ShapeDtypeStruct((rows, EDGE), jnp.float32),
            jax.ShapeDtypeStruct((EDGE, cols), jnp.float32),
            jax.ShapeDtypeStruct((EDGE, EDGE), jnp.float32),
        ),
        in_specs=[pl.BlockSpec(memory_space=pl.ANY)],
        out_specs=(pl.BlockSpec(memory_space=pl.ANY),) * 3,
        scratch_shapes=[
            pltpu.SemaphoreType.DMA((STEPS, chunks, 2 + width)),
            pltpu.SemaphoreType.DMA((STEPS, chunks)),
            pltpu.SemaphoreType.DMA((row_count,)),
            pltpu.SemaphoreType.DMA((STEPS,)),
            pltpu.SemaphoreType.DMA((row_count,)),
            pltpu.SemaphoreType.DMA((STEPS,)),
            pltpu.SemaphoreType.DMA((3,)),
        ],
        compiler_params=pltpu.CompilerParams(collective_id=0, has_side_effects=True),
    )(kernel)


def invert_base(block, out_ref):
    tiles = [block[8 * t : 8 * t + 8, :] for t in range(BASE // 8)]
    row_ids = lax.broadcasted_iota(jnp.int32, (8, BASE), 0)
    lane_ids = lax.broadcasted_iota(jnp.int32, (8, BASE), 1)
    aug = [(row_ids + 8 * t == lane_ids).astype(jnp.float32) for t in range(BASE // 8)]

    def row(tile, r):
        return jnp.broadcast_to(tile[r : r + 1, :], (8, BASE))

    for j in range(0, BASE, 2):
        t0, r = j // 8, j % 8
        live = range(t0, BASE // 8)
        first = {t: jnp.broadcast_to(tiles[t][:, j : j + 1], (8, BASE)) for t in live}
        second = {t: jnp.broadcast_to(tiles[t][:, j + 1 : j + 2], (8, BASE)) for t in live}
        d00 = row(first[t0], r)
        d01 = row(second[t0], r)
        d11 = row(second[t0], r + 1)
        i00 = 1.0 / d00
        ratio = d01 * i00
        d11 = d11 - d01 * ratio
        i11 = 1.0 / d11
        a0, a1 = row(tiles[t0], r), row(tiles[t0], r + 1)
        b0, b1 = row(aug[t0], r), row(aug[t0], r + 1)
        a1 = a1 - ratio * a0
        b1 = b1 - ratio * b0
        out_ref[j : j + 1, :] = (b0 * lax.rsqrt(d00))[0:1, :]
        out_ref[j + 1 : j + 2, :] = (b1 * lax.rsqrt(d11))[0:1, :]
        u1 = a1 * i11
        u0 = a0 * i00 - ratio * u1
        v1 = b1 * i11
        v0 = b0 * i00 - ratio * v1
        for t in live:
            tiles[t] = tiles[t] - first[t] * u0 - second[t] * u1
            aug[t] = aug[t] - first[t] * v0 - second[t] * v1


def factor_kernel(c_ref, out_ref, g_ref, w_ref, d_ref):
    for i in range(STEPS):
        rows = slice(i * BLOCK, (i + 1) * BLOCK)
        g_ref[rows, rows] = c_ref[rows, rows]
        for k in range(i):
            cols = slice(k * BLOCK, (k + 1) * BLOCK)
            g_ref[cols, rows] = c_ref[rows, cols].T
            g_ref[rows, cols] = jnp.zeros((BLOCK, BLOCK), jnp.float32)

    @pl.loop(0, EDGE // BASE)
    def _(step):
        here = pl.ds(pl.multiple_of(step * BASE, BASE), BASE)
        invert_base(g_ref[here, here], d_ref)
        inverse = d_ref[...]
        w_ref[...] = jnp.dot(
            inverse, g_ref[here, :], precision=lax.Precision.HIGHEST, preferred_element_type=jnp.float32
        )
        w_ref[:, here] = inverse
        col_ids = lax.broadcasted_iota(jnp.int32, (BASE, EDGE), 1)
        out_ref[here, :] = jnp.where(col_ids < (step + 1) * BASE, w_ref[...], 0.0)

        @pl.loop(step + 1, EDGE // BASE)
        def _(below):
            there = pl.ds(pl.multiple_of(below * BASE, BASE), BASE)
            g_ref[there, here] = jnp.zeros((BASE, BASE), jnp.float32)
            g_ref[there, :] -= jnp.dot(
                w_ref[:, there].T, w_ref[...], precision=lax.Precision.HIGHEST, preferred_element_type=jnp.float32
            )


def factor(corner):
    return pl.pallas_call(
        factor_kernel,
        out_shape=jax.ShapeDtypeStruct((EDGE, EDGE), jnp.float32),
        in_specs=[pl.BlockSpec(memory_space=pltpu.VMEM)],
        out_specs=pl.BlockSpec(memory_space=pltpu.VMEM),
        scratch_shapes=[
            pltpu.VMEM((EDGE, EDGE), jnp.float32),
            pltpu.VMEM((BASE, EDGE), jnp.float32),
            pltpu.VMEM((BASE, BASE), jnp.float32),
        ],
        compiler_params=pltpu.CompilerParams(vmem_limit_bytes=32 * 1024 * 1024),
    )(corner)


def shards(kernel):
    row_count = lax.axis_size("row")
    col_count = lax.axis_size("col")
    row_index = lax.axis_index("row")
    col_index = lax.axis_index("col")
    rows_local, cols_local = kernel.shape
    row_ids = jnp.arange(rows_local) // BLOCK * row_count + row_index
    col_ids = jnp.arange(cols_local) // BLOCK * col_count + col_index
    slabs, edge, corner = gather(kernel, row_count, col_count)
    inverse = factor(corner)
    dot = functools.partial(lax.dot_general, precision=lax.Precision.HIGH, preferred_element_type=jnp.float32)
    panel = dot(slabs, inverse, (((1,), (1,)), ((), ())))
    row_places = row_ids * BLOCK + jnp.arange(rows_local) % BLOCK
    panel = jnp.where(row_places[:, None] >= jnp.arange(EDGE)[None, :], panel, jnp.float32(0.0))
    across = dot(inverse, edge, (((1,), (0,)), ((), ())))
    update = dot(panel, across, (((1,), (0,)), ((), ())))
    keep = (row_ids >= STEPS)[:, None] & (col_ids >= STEPS)[None, :]
    schur = jnp.where(keep, kernel - update, jnp.float32(0.0))
    return (schur, panel)


def solution(mesh):
    return jax.shard_map(
        shards,
        mesh=mesh,
        in_specs=(P("row", "col"),),
        out_specs=(P("row", "col"), P("row", None)),
        check_vma=False,
    )
```

time: 840 us -> 253 us (0.30); the launches traced: 830 us -> 253 us
  waiting for transfers between devices: 490 us -> 0 us
  Pallas kernels: 0 us -> 216 us
  other arithmetic: 195 us -> 0.03 us
  local copies, waits for them, and re-layouts: 74.3 us -> 1.66 us
  between operations: 18.8 us -> 0.67 us
  matrix products: 49.9 us -> 34.1 us
    psum x9 -> x0, waiting for transfers between devices: 490 us -> none  [spread(): return lax.psum(jnp.where(mine, array, jnp.zeros_like(array)), axis)]
    pallas_call x0 -> x2, Pallas kernels: none -> 216 us  [the longest x1 146 us: gather(): pl.pallas_call(functools.partial(gather_kernel, row_count, col_count), ou...]
    another operation x27 -> x0, other arithmetic: 165 us -> none  [the longest x20 103 us: shards(): factor = jnp.linalg.cholesky(corner)]
    unnamed x27 -> x4, local copies, waits for them, and re-layouts: 38.8 us -> 1.66 us
    select_n x9 -> x0, other arithmetic: 20.7 us -> none  [spread(): return lax.psum(jnp.where(mine, array, jnp.zeros_like(array)), axis)]
    another operation x15 -> x0, matrix products: 16.3 us -> none  [the longest x9 14.8 us: place(): solved = jax.scipy.linalg.solve_triangular(factor, column.T, lower=True).T]
    another operation x31 -> x0, local copies, waits for them, and re-layouts: 12.5 us -> none  [the longest x22 12 us: place(): solved = jax.scipy.linalg.solve_triangular(factor, column.T, lower=True).T]
    reshape x3 -> x0, local copies, waits for them, and re-layouts: 11.2 us -> none  [pick(): grouped = panel.reshape(col_blocks, groups, width, width)]
  transfers between devices with their start and end apart: 9 -> 0, of which waited for: 9 -> 0; matrix products, arithmetic and copies ran while one was open for 2% -> 0% of each run, Pallas kernels for 0% -> 0%
where the time goes in v1:
time: 253 us
  Pallas kernels  216 us (85%)
  matrix products  34.1 us (13%)
    pallas_call x1, Pallas kernels, gather(): pl.pallas_call(functools.partial(gather_kernel, row_count, col_count), ou...  146 us
    pallas_call x1, Pallas kernels, factor(): pl.pallas_call(factor_kernel, out_shape=jax.ShapeDtypeStruct((EDGE, EDGE)...  70.4 us
    dot_general x1, matrix products, shards(): update = dot(panel, across, (((1,), (0,)), ((), ())))  16.6 us
    dot_general x1, matrix products, shards(): panel = dot(slabs, inverse, (((1,), (1,)), ((), ())))  11.9 us
    dot_general x1, matrix products, shards(): across = dot(inverse, edge, (((1,), (0,)), ((), ())))  5.66 us

profile of v1, /device:TPU:24, one launch (start us, length us, event | category | flops | bytes accessed | tf_op | source)
XLA Modules:
  0.0 252.6 jit_solution(6070247740740880196)
XLA Ops:
  0.6 145.7 %shard_map.30 = (f32[2048,768]{1,0:T(8,128)}, f32[768,1024]{1,0:T(8,128)}, f32[768,768]{1,0:T(8,128)}) custom-call(f32[2048,1024]{1,0:T(8,128)} %m_ref.1), custom_call_target="tpu_custom_call" | custom-call | tf_op jit(solution)/shard_map/pallas_call | solution.py:209
  146.3 0.0 copy-start
  146.3 1.7 copy-done
  148.0 70.4 %shard_map.31 = f32[768,768]{1,0:T(8,128)S(1)} custom-call(f32[768,768]{1,0:T(8,128)S(1)} %copy-done), custom_call_target="tpu_custom_call" | custom-call | tf_op jit(solution)/shard_map/pallas_call | solution.py:298
  218.4 0.0 copy-start.1
  218.4 11.9 %fusion = f32[2048,768]{1,0:T(8,128)} fusion(f32[2048,768]{1,0:T(8,128)} %get-tuple-element.5, f32[768,768]{1,0:T(8,128)S(1)} %shard_map.31, s32[2048]{0:T(1024)S(1)} %fusion.9), kind=kOutput, calls=%fused_computation.2 | convolution fusion | flops 7250903040 | bytes 14950400 | tf_op jit(solution)/shard_map/dot_general | solution.py:323
  230.3 0.0 copy-done.1
  230.3 5.7 %fusion.19 = f32[768,1024]{1,0:T(8,128)} fusion(f32[768,768]{1,0:T(8,128)S(1)} %shard_map.31, f32[768,1024]{1,0:T(8,128)S(1)} %copy-done.1), kind=kOutput, calls=%fused_computation.29 | convolution fusion | flops 3623878656 | bytes 8650752 | tf_op jit(solution)/shard_map/dot_general | solution.py:326
  236.0 16.6 %subtract_select_fusion = f32[2048,1024]{1,0:T(8,128)} fusion(f32[2048,1024]{1,0:T(8,128)} %m_ref.1, pred[1024]{0:T(1024)(128)(4,1)S(1)} %fusion.15, pred[2048]{0:T(1024)(128)(4,1)S(1)} %fusion.12, f32[2048,768]{1,0:T(8,128)} %fusion, f32[768,1024]{1,0:T(8,128)} %fusion.19), kind=kOutput, calls=%fused_computation | convolution fusion | flops 9669967872 | bytes 26217472 | tf_op jit(solution)/shard_map/dot_general | solution.py:327
  (3 shorter events, 0.0 us)
Async XLA Ops:
  146.3 1.7 copy-start
  218.4 11.9 %copy-start.1 = (f32[768,1024]{1,0:T(8,128)S(1)}, f32[768,1024]{1,0:T(8,128)}, u32[]{:S(2)}) copy-start(f32[768,1024]{1,0:T(8,128)} %get-tuple-element.7) | copy-start | bytes 9437188

commit v2 on v1

--- a/solution.py
+++ b/solution.py
@@ -22,8 +22,8 @@
     return width
 
 
-def gather_kernel(row_count, col_count, m_ref, a_ref, r_ref, c_ref, slab_send, slab_recv, edge_send, edge_recv,
-                  corner_send, corner_recv, local_sem):
+def gather_kernel(row_count, col_count, m_ref, a_ref, r_ref, out_ref, c_ref, g_ref, w_ref, d_ref, slab_send, slab_recv,
+                  edge_send, edge_recv, corner_send, corner_recv, local_sem):
     width = line_width(col_count)
     depth = col_count // width
     rows = m_ref.shape[0]
@@ -174,7 +174,23 @@
             for other in range(1, row_count):
                 edge_copy(i, other).start()
 
-    @pl.loop(lead_rounds, rounds)
+    for i in range(STEPS):
+        @pl.when(p == i)
+        def _():
+            local_corner(i).wait()
+
+        @pl.when(p != i)
+        def _():
+            corner_copy(i, 1).wait_recv()
+
+    def between(step):
+        @pl.when(step + lead_rounds < rounds)
+        def _():
+            relay(step + lead_rounds)
+
+    factor_corner(c_ref, out_ref, g_ref, w_ref, d_ref, between)
+
+    @pl.loop(lead_rounds + EDGE // BASE, rounds)
     def _(step):
         relay(step)
 
@@ -185,7 +201,6 @@
     for i in range(STEPS):
         @pl.when(p == i)
         def _():
-            local_corner(i).wait()
             local_edge(i).wait()
             for other in range(1, row_count):
                 corner_copy(i, other).wait_send()
@@ -193,7 +208,6 @@
 
         @pl.when(p != i)
         def _():
-            corner_copy(i, 1).wait_recv()
             edge_copy(i, 1).wait_recv()
 
     for k in range(STEPS):
@@ -214,8 +228,16 @@
             jax.ShapeDtypeStruct((EDGE, EDGE), jnp.float32),
         ),
         in_specs=[pl.BlockSpec(memory_space=pl.ANY)],
-        out_specs=(pl.BlockSpec(memory_space=pl.ANY),) * 3,
+        out_specs=(
+            pl.BlockSpec(memory_space=pl.ANY),
+            pl.BlockSpec(memory_space=pl.ANY),
+            pl.BlockSpec(memory_space=pltpu.VMEM),
+        ),
         scratch_shapes=[
+            pltpu.VMEM((EDGE, EDGE), jnp.float32),
+            pltpu.VMEM((EDGE, EDGE), jnp.float32),
+            pltpu.VMEM((BASE, EDGE), jnp.float32),
+            pltpu.VMEM((BASE, BASE), jnp.float32),
             pltpu.SemaphoreType.DMA((STEPS, chunks, 2 + width)),
             pltpu.SemaphoreType.DMA((STEPS, chunks)),
             pltpu.SemaphoreType.DMA((row_count,)),
@@ -224,7 +246,9 @@
             pltpu.SemaphoreType.DMA((STEPS,)),
             pltpu.SemaphoreType.DMA((3,)),
         ],
-        compiler_params=pltpu.CompilerParams(collective_id=0, has_side_effects=True),
+        compiler_params=pltpu.CompilerParams(
+            collective_id=0, has_side_effects=True, vmem_limit_bytes=32 * 1024 * 1024
+        ),
     )(kernel)
 
 
@@ -264,7 +288,7 @@
             aug[t] = aug[t] - first[t] * v0 - second[t] * v1
 
 
-def factor_kernel(c_ref, out_ref, g_ref, w_ref, d_ref):
+def factor_corner(c_ref, out_ref, g_ref, w_ref, d_ref, between):
     for i in range(STEPS):
         rows = slice(i * BLOCK, (i + 1) * BLOCK)
         g_ref[rows, rows] = c_ref[rows, rows]
@@ -275,6 +299,7 @@
 
     @pl.loop(0, EDGE // BASE)
     def _(step):
+        between(step)
         here = pl.ds(pl.multiple_of(step * BASE, BASE), BASE)
         invert_base(g_ref[here, here], d_ref)
         inverse = d_ref[...]
@@ -292,21 +317,6 @@
             g_ref[there, :] -= jnp.dot(
                 w_ref[:, there].T, w_ref[...], precision=lax.Precision.HIGHEST, preferred_element_type=jnp.float32
             )
-
-
-def factor(corner):
-    return pl.pallas_call(
-        factor_kernel,
-        out_shape=jax.ShapeDtypeStruct((EDGE, EDGE), jnp.float32),
-        in_specs=[pl.BlockSpec(memory_space=pltpu.VMEM)],
-        out_specs=pl.BlockSpec(memory_space=pltpu.VMEM),
-        scratch_shapes=[
-            pltpu.VMEM((EDGE, EDGE), jnp.float32),
-            pltpu.VMEM((BASE, EDGE), jnp.float32),
-            pltpu.VMEM((BASE, BASE), jnp.float32),
-        ],
-        compiler_params=pltpu.CompilerParams(vmem_limit_bytes=32 * 1024 * 1024),
-    )(corner)
 
 
 def shards(kernel):
@@ -317,8 +327,7 @@
     rows_local, cols_local = kernel.shape
     row_ids = jnp.arange(rows_local) // BLOCK * row_count + row_index
     col_ids = jnp.arange(cols_local) // BLOCK * col_count + col_index
-    slabs, edge, corner = gather(kernel, row_count, col_count)
-    inverse = factor(corner)
+    slabs, edge, inverse = gather(kernel, row_count, col_count)
     dot = functools.partial(lax.dot_general, precision=lax.Precision.HIGH, preferred_element_type=jnp.float32)
     panel = dot(slabs, inverse, (((1,), (1,)), ((), ())))
     row_places = row_ids * BLOCK + jnp.arange(rows_local) % BLOCK

time: 253 us -> 253 us (level)
  Pallas kernels: 216 us -> 210 us
  local copies, waits for them, and re-layouts: 1.66 us -> 7.5 us
    pallas_call x1 -> x0, Pallas kernels: 70.4 us -> none  [factor(): pl.pallas_call(factor_kernel, out_shape=jax.ShapeDtypeStruct((EDGE, EDGE)...]
    pallas_call x1, Pallas kernels: 146 us -> 210 us  [gather(): pl.pallas_call(functools.partial(gather_kernel, row_count, col_count), ou...]
    unnamed x4 -> x8, local copies, waits for them, and re-layouts: 1.66 us -> 7.5 us
where the time goes in v2:
time: 253 us
  Pallas kernels  210 us (83%)
  matrix products  34.9 us (14%)
  local copies, waits for them, and re-layouts  7.5 us (3%)
    pallas_call x1, Pallas kernels, gather(): pl.pallas_call(functools.partial(gather_kernel, row_count, col_count), ou...  210 us
    dot_general x1, matrix products, shards(): update = dot(panel, across, (((1,), (0,)), ((), ())))  16.8 us
    dot_general x1, matrix products, shards(): panel = dot(slabs, inverse, (((1,), (1,)), ((), ())))  12.6 us
    unnamed x8, local copies, waits for them, and re-layouts  7.5 us
    dot_general x1, matrix products, shards(): across = dot(inverse, edge, (((1,), (0,)), ((), ())))  5.52 us

profile of v2, /device:TPU:24, one launch (start us, length us, event | category | flops | bytes accessed | tf_op | source)
XLA Modules:
  0.0 253.1 jit_solution(6691082440658933198)
XLA Ops:
  0.6 0.0 copy-start
  0.6 3.4 %copy-done = f32[2048,1024]{1,0:T(8,128)S(1)} copy-done((f32[2048,1024]{1,0:T(8,128)S(1)}, f32[2048,1024]{1,0:T(8,128)}, u32[]{:S(2)}) %copy-start) | copy-done | bytes 8388632
  4.0 210.0 %shard_map.30 = (f32[2048,768]{1,0:T(8,128)S(1)}, f32[768,1024]{1,0:T(8,128)S(1)}, f32[768,768]{1,0:T(8,128)S(1)}) custom-call(f32[2048,1024]{1,0:T(8,128)S(1)} %copy-done), custom_call_target="tpu_custom_call" | custom-call | tf_op jit(solution)/shard_map/pallas_call | solution.py:223
  214.0 0.0 copy-start.1
  214.0 1.4 copy-done.1
  215.4 0.0 copy-start.3
  215.4 2.7 %copy-done.3 = f32[2048,768]{1,0:T(8,128)} copy-done((f32[2048,768]{1,0:T(8,128)}, f32[2048,768]{1,0:T(8,128)S(1)}, u32[]{:S(2)}) %copy-start.3) | copy-done | bytes 6291480
  218.1 0.0 copy-start.2
  218.1 12.6 %fusion = f32[2048,768]{1,0:T(8,128)} fusion(f32[2048,768]{1,0:T(8,128)} %copy-done.3, f32[768,768]{1,0:T(8,128)} %copy-done.1, s32[2048]{0:T(1024)S(1)} %fusion.9), kind=kOutput, calls=%fused_computation.2 | convolution fusion | flops 7250903040 | bytes 14950400 | tf_op jit(solution)/shard_map/dot_general | solution.py:332
  230.7 0.0 copy-done.2
  230.7 5.5 %fusion.19 = f32[768,1024]{1,0:T(8,128)} fusion(f32[768,768]{1,0:T(8,128)S(1)} %copy-done.2, f32[768,1024]{1,0:T(8,128)S(1)} %get-tuple-element.7), kind=kOutput, calls=%fused_computation.29 | convolution fusion | flops 3623878656 | bytes 8650752 | tf_op jit(solution)/shard_map/dot_general | solution.py:335
  236.3 16.8 %subtract_select_fusion = f32[2048,1024]{1,0:T(8,128)} fusion(f32[2048,1024]{1,0:T(8,128)} %m_ref.1, pred[1024]{0:T(1024)(128)(4,1)S(1)} %fusion.15, pred[2048]{0:T(1024)(128)(4,1)S(1)} %fusion.12, f32[2048,768]{1,0:T(8,128)} %fusion, f32[768,1024]{1,0:T(8,128)} %fusion.19), kind=kOutput, calls=%fused_computation | convolution fusion | flops 9669967872 | bytes 26217472 | tf_op jit(solution)/shard_map/dot_general | solution.py:336
  (3 shorter events, 0.0 us)
Async XLA Ops:
  0.6 3.4 %copy-start = (f32[2048,1024]{1,0:T(8,128)S(1)}, f32[2048,1024]{1,0:T(8,128)}, u32[]{:S(2)}) copy-start(f32[2048,1024]{1,0:T(8,128)} %m_ref.1) | copy-start | bytes 25165828
  214.0 1.4 copy-start.1
  215.4 2.7 %copy-start.3 = (f32[2048,768]{1,0:T(8,128)}, f32[2048,768]{1,0:T(8,128)S(1)}, u32[]{:S(2)}) copy-start(f32[2048,768]{1,0:T(8,128)S(1)} %get-tuple-element.5) | copy-start | bytes 18874372
  218.1 12.6 %copy-start.2 = (f32[768,768]{1,0:T(8,128)S(1)}, f32[768,768]{1,0:T(8,128)}, u32[]{:S(2)}) copy-start(f32[768,768]{1,0:T(8,128)} %copy-done.1) | copy-start | bytes 7077892

commit v3 on v2

--- a/solution.py
+++ b/solution.py
@@ -99,11 +99,13 @@
                 m_ref.at[:, pl.ds(0, BLOCK)], a_ref.at[:, pl.ds(k * BLOCK, BLOCK)], local_sem.at[0]
             ).start()
 
-            @pl.loop(0, chunks)
-            def _(chunk):
-                forward(k, chunk, lambda copy: copy.start())
-
     def relay(step):
+        for k in range(STEPS):
+            @pl.when(q == k)
+            def _():
+                for part in range(width):
+                    forward(k, step * width + part, lambda copy: copy.start())
+
         for k in range(STEPS):
             chunk = step * width + b
 
@@ -142,15 +144,23 @@
             device_id_type=MESH,
         )
 
-    def edge_copy(i, other):
+    def edge_copy(i, other, piece):
+        start = pl.multiple_of(piece * (BLOCK // rounds), BLOCK // rounds)
         return pltpu.make_async_remote_copy(
-            src_ref=m_ref.at[pl.ds(0, BLOCK), :],
-            dst_ref=r_ref.at[pl.ds(i * BLOCK, BLOCK), :],
-            send_sem=edge_send.at[other],
-            recv_sem=edge_recv.at[i],
+            src_ref=m_ref.at[pl.ds(start, BLOCK // rounds), :],
+            dst_ref=r_ref.at[pl.ds(i * BLOCK + start, BLOCK // rounds), :],
+            send_sem=edge_send.at[other, piece],
+            recv_sem=edge_recv.at[i, piece],
             device_id=(lax.rem(p + other, row_count), q),
             device_id_type=MESH,
         )
+
+    def edge_round(piece):
+        for i in range(STEPS):
+            @pl.when(p == i)
+            def _():
+                for other in range(1, row_count):
+                    edge_copy(i, other, piece).start()
 
     def local_corner(i):
         return pltpu.make_async_copy(
@@ -171,8 +181,9 @@
             local_edge(i).start()
             for other in range(1, row_count):
                 corner_copy(i, other).start()
-            for other in range(1, row_count):
-                edge_copy(i, other).start()
+
+    for step in range(lead_rounds):
+        edge_round(jnp.int32(step))
 
     for i in range(STEPS):
         @pl.when(p == i)
@@ -187,12 +198,14 @@
         @pl.when(step + lead_rounds < rounds)
         def _():
             relay(step + lead_rounds)
+            edge_round(step + lead_rounds)
 
     factor_corner(c_ref, out_ref, g_ref, w_ref, d_ref, between)
 
     @pl.loop(lead_rounds + EDGE // BASE, rounds)
     def _(step):
         relay(step)
+        edge_round(step)
 
     @pl.loop(lead_rounds, rounds)
     def _(step):
@@ -204,11 +217,17 @@
             local_edge(i).wait()
             for other in range(1, row_count):
                 corner_copy(i, other).wait_send()
-                edge_copy(i, other).wait_send()
+
+            @pl.loop(0, rounds)
+            def _(piece):
+                for other in range(1, row_count):
+                    edge_copy(i, other, piece).wait_send()
 
         @pl.when(p != i)
         def _():
-            edge_copy(i, 1).wait_recv()
+            @pl.loop(0, rounds)
+            def _(piece):
+                edge_copy(i, 1, piece).wait_recv()
 
     for k in range(STEPS):
         @pl.loop(0, chunks)
@@ -240,8 +259,8 @@
             pltpu.VMEM((BASE, BASE), jnp.float32),
             pltpu.SemaphoreType.DMA((STEPS, chunks, 2 + width)),
             pltpu.SemaphoreType.DMA((STEPS, chunks)),
-            pltpu.SemaphoreType.DMA((row_count,)),
-            pltpu.SemaphoreType.DMA((STEPS,)),
+            pltpu.SemaphoreType.DMA((row_count, chunks // width)),
+            pltpu.SemaphoreType.DMA((STEPS, chunks // width)),
             pltpu.SemaphoreType.DMA((row_count,)),
             pltpu.SemaphoreType.DMA((STEPS,)),
             pltpu.SemaphoreType.DMA((3,)),

time: 253 us -> 242 us (0.957)
  Pallas kernels: 210 us -> 198 us
    pallas_call x1, Pallas kernels: 210 us -> 198 us  [gather(): pl.pallas_call(functools.partial(gather_kernel, row_count, col_count), ou...]
where the time goes in v3:
time: 242 us; the launch traced here: 241 us
  Pallas kernels  198 us (82%)
  matrix products  34.9 us (14%)
  local copies, waits for them, and re-layouts  7.5 us (3%)
    pallas_call x1, Pallas kernels, gather(): pl.pallas_call(functools.partial(gather_kernel, row_count, col_count), ou...  198 us
    dot_general x1, matrix products, shards(): update = dot(panel, across, (((1,), (0,)), ((), ())))  16.8 us
    dot_general x1, matrix products, shards(): panel = dot(slabs, inverse, (((1,), (1,)), ((), ())))  12.6 us
    unnamed x8, local copies, waits for them, and re-layouts  7.5 us
    dot_general x1, matrix products, shards(): across = dot(inverse, edge, (((1,), (0,)), ((), ())))  5.52 us

profile of v3, /device:TPU:24, one launch (start us, length us, event | category | flops | bytes accessed | tf_op | source)
XLA Modules:
  0.0 241.3 jit_solution(13368895474767269392)
XLA Ops:
  0.6 0.0 copy-start
  0.6 3.4 %copy-done = f32[2048,1024]{1,0:T(8,128)S(1)} copy-done((f32[2048,1024]{1,0:T(8,128)S(1)}, f32[2048,1024]{1,0:T(8,128)}, u32[]{:S(2)}) %copy-start) | copy-done | bytes 8388632
  4.0 198.3 %shard_map.30 = (f32[2048,768]{1,0:T(8,128)S(1)}, f32[768,1024]{1,0:T(8,128)S(1)}, f32[768,768]{1,0:T(8,128)S(1)}) custom-call(f32[2048,1024]{1,0:T(8,128)S(1)} %copy-done), custom_call_target="tpu_custom_call" | custom-call | tf_op jit(solution)/shard_map/pallas_call | solution.py:242
  202.3 0.0 copy-start.1
  202.3 1.4 copy-done.1
  203.7 0.0 copy-start.3
  203.7 2.7 %copy-done.3 = f32[2048,768]{1,0:T(8,128)} copy-done((f32[2048,768]{1,0:T(8,128)}, f32[2048,768]{1,0:T(8,128)S(1)}, u32[]{:S(2)}) %copy-start.3) | copy-done | bytes 6291480
  206.4 0.0 copy-start.2
  206.4 12.6 %fusion = f32[2048,768]{1,0:T(8,128)} fusion(f32[2048,768]{1,0:T(8,128)} %copy-done.3, f32[768,768]{1,0:T(8,128)} %copy-done.1, s32[2048]{0:T(1024)S(1)} %fusion.9), kind=kOutput, calls=%fused_computation.2 | convolution fusion | flops 7250903040 | bytes 14950400 | tf_op jit(solution)/shard_map/dot_general | solution.py:351
  219.0 0.0 copy-done.2
  219.0 5.5 %fusion.19 = f32[768,1024]{1,0:T(8,128)} fusion(f32[768,768]{1,0:T(8,128)S(1)} %copy-done.2, f32[768,1024]{1,0:T(8,128)S(1)} %get-tuple-element.7), kind=kOutput, calls=%fused_computation.29 | convolution fusion | flops 3623878656 | bytes 8650752 | tf_op jit(solution)/shard_map/dot_general | solution.py:354
  224.5 16.8 %subtract_select_fusion = f32[2048,1024]{1,0:T(8,128)} fusion(f32[2048,1024]{1,0:T(8,128)} %m_ref.1, pred[1024]{0:T(1024)(128)(4,1)S(1)} %fusion.15, pred[2048]{0:T(1024)(128)(4,1)S(1)} %fusion.12, f32[2048,768]{1,0:T(8,128)} %fusion, f32[768,1024]{1,0:T(8,128)} %fusion.19), kind=kOutput, calls=%fused_computation | convolution fusion | flops 9669967872 | bytes 26217472 | tf_op jit(solution)/shard_map/dot_general | solution.py:355
  (3 shorter events, 0.0 us)
Async XLA Ops:
  0.6 3.4 %copy-start = (f32[2048,1024]{1,0:T(8,128)S(1)}, f32[2048,1024]{1,0:T(8,128)}, u32[]{:S(2)}) copy-start(f32[2048,1024]{1,0:T(8,128)} %m_ref.1) | copy-start | bytes 25165828
  202.3 1.4 copy-start.1
  203.7 2.7 %copy-start.3 = (f32[2048,768]{1,0:T(8,128)}, f32[2048,768]{1,0:T(8,128)S(1)}, u32[]{:S(2)}) copy-start(f32[2048,768]{1,0:T(8,128)S(1)} %get-tuple-element.5) | copy-start | bytes 18874372
  206.4 12.6 %copy-start.2 = (f32[768,768]{1,0:T(8,128)S(1)}, f32[768,768]{1,0:T(8,128)}, u32[]{:S(2)}) copy-start(f32[768,768]{1,0:T(8,128)} %copy-done.1) | copy-start | bytes 7077892
